TPU v7x, 512 devices: a whole 4x4x16 slice. The times are simulated.
512 devices in a mesh: expert: 128 (over y, z, core), half: 4 (over x).
Axes of the slice: x: 4, y: 4, z: 16, core: 2. Of those that a mesh axis runs over, the one named last changes fastest.
Arguments:
- tokens: bfloat16 [2048, 2048], P('expert', 'half'), may hold values from -6 to 6
- upstream: bfloat16 [2048, 2048], P('expert', 'half'), may hold values from -6 to 6
- expert_ids: int32 [2048, 8], P('expert'), may hold values from 0 to 127, all different within a row; in each aligned block of 16 rows (0 to 15, 16 to 31, ...) at most 2 rows name the same one
- gate_probs: float32 [2048, 8], P('expert'), may hold values from 0.01 to 1
- pad_mask: int32 [2048], P('expert'), may hold values 0 or 1
- gate_weight: bfloat16 [128, 2048, 1536], P('expert', None, 'half'), may hold values from -0.125 to 0.125
- up_weight: bfloat16 [128, 2048, 1536], P('expert', None, 'half'), may hold values from -0.125 to 0.125
- down_weight: bfloat16 [128, 1536, 2048], P('expert', 'half'), may hold values from -0.15625 to 0.15625
Outputs:
- layer_out: bfloat16 [2048, 2048], P('expert', 'half')
- grad_tokens: bfloat16 [2048, 2048], P('expert', 'half')
Inputs may be any that keep to these rules, and one draw needn't show every extreme that they name: `expert_ids`: each row names 8 different experts. In the rows of one device (aligned blocks of 16 rows) no expert is named more than 2 times, a bound that some block reaches.
All inputs are finite; a program needn't handle non-finite values. No bound on the sum of `pad_mask` on one device may be relied on, other than what follows from the above.
Results may differ from a plain program's by a relative error of at most 0.025.
Values may be sent and summed in bfloat16 or wider, within the bound.
No kernel may reach another device: no remote copies, remote signals or barrier semaphores. Data moves between devices by JAX's collectives and lax.ppermute only.
A program may use at most 64 MiB of HBM per device.

v0:
```python
import math
import jax
import jax.numpy as jnp
from jax import lax
from jax.sharding import PartitionSpec as P

orth_weight = 0.25


def assign_slots(expert_ids, experts, capacity):
    tok_count, top_count = expert_ids.shape
    flat_ids = expert_ids.reshape(tok_count * top_count)
    onehot = (flat_ids[:, None] == jnp.arange(experts, dtype=jnp.int32)[None, :]).astype(jnp.int32)
    before = jnp.cumsum(onehot, axis=0) - onehot
    slot_index = jnp.sum(before * onehot, axis=1)
    return flat_ids * capacity + slot_index


def placement_matrix(slot_dest, slots_total):
    row_index = jnp.arange(slots_total, dtype=jnp.int32)
    return (row_index[:, None] == slot_dest[None, :]).astype(jnp.bfloat16)


def to_experts(place, items):
    whole = lax.all_gather(items, "half", axis=1, tiled=True)
    buckets = jnp.dot(place, whole, preferred_element_type=jnp.float32).astype(jnp.bfloat16)
    return lax.all_to_all(buckets, "expert", split_axis=0, concat_axis=0, tiled=True)


def to_homes(partial_value):
    summed = lax.psum_scatter(
        partial_value.astype(jnp.bfloat16), "half", scatter_dimension=1, tiled=True
    )
    return lax.all_to_all(summed, "expert", split_axis=0, concat_axis=0, tiled=True)


def shards(tokens, upstream, expert_ids, gate_probs, pad_mask, gate_weight, up_weight, down_weight):
    tok_count, top_count = expert_ids.shape
    experts = lax.axis_size("expert")
    capacity = min(tok_count, 2 * tok_count * top_count // experts)
    slots_total = experts * capacity
    full_width = tokens.shape[1] * lax.axis_size("half")
    slot_dest = assign_slots(expert_ids, experts, capacity)
    place_items = placement_matrix(slot_dest, slots_total)
    place_tokens = jnp.sum(place_items.reshape(slots_total, tok_count, top_count), axis=2)
    weight_gate = gate_weight[0]
    weight_up = up_weight[0]
    weight_down = down_weight[0]
    rows_in = to_experts(place_tokens, tokens)
    gate_val = jnp.dot(rows_in, weight_gate, preferred_element_type=jnp.float32)
    up_val = jnp.dot(rows_in, weight_up, preferred_element_type=jnp.float32)
    hidden_act = (jax.nn.silu(gate_val) * up_val).astype(jnp.bfloat16)
    partial_value = jnp.dot(hidden_act, weight_down, preferred_element_type=jnp.float32)
    out_home = to_homes(partial_value)
    outputs = jnp.take(out_home, slot_dest, axis=0).reshape(tok_count, top_count, -1)
    out_float = outputs.astype(jnp.float32)
    shares = gate_probs / jnp.sum(gate_probs, axis=1, keepdims=True)
    layer_out = jnp.sum(shares[:, :, None] * out_float, axis=1).astype(jnp.bfloat16)
    gram_part = jnp.einsum("tjd,tkd->tjk", out_float, out_float) / math.sqrt(full_width)
    gram = lax.psum(gram_part, "half")
    off_diag = 1.0 - jnp.eye(top_count, dtype=jnp.float32)
    coeffs = orth_weight * gram * off_diag
    grad_out = pad_mask.astype(jnp.float32)[:, None, None] * (
        shares[:, :, None] * upstream.astype(jnp.float32)[:, None, :]
        + jnp.einsum("tjk,tkd->tjd", coeffs, out_float)
    )
    grad_items = grad_out.astype(jnp.bfloat16).reshape(tok_count * top_count, -1)
    grad_rows = to_experts(place_items, grad_items)
    grad_act = jnp.einsum("rd,hd->rh", grad_rows, weight_down, preferred_element_type=jnp.float32)
    sigma = jax.nn.sigmoid(gate_val)
    grad_gate = (grad_act * up_val * sigma * (1.0 + gate_val * (1.0 - sigma))).astype(jnp.bfloat16)
    grad_up = (grad_act * gate_val * sigma).astype(jnp.bfloat16)
    grad_partial = jnp.einsum(
        "rh,dh->rd", grad_gate, weight_gate, preferred_element_type=jnp.float32
    )
    grad_partial = grad_partial + jnp.einsum(
        "rh,dh->rd", grad_up, weight_up, preferred_element_type=jnp.float32
    )
    grad_home = to_homes(grad_partial)
    grad_pairs = jnp.take(grad_home, slot_dest, axis=0).reshape(tok_count, top_count, -1)
    grad_tokens = jnp.sum(grad_pairs.astype(jnp.float32), axis=1).astype(jnp.bfloat16)
    return (layer_out, grad_tokens)


def solution(mesh):
    in_specs = (
        P("expert", "half"),
        P("expert", "half"),
        P("expert", None),
        P("expert", None),
        P("expert"),
        P("expert", None, "half"),
        P("expert", None, "half"),
        P("expert", "half", None),
    )
    out_specs = (P("expert", "half"), P("expert", "half"))
    return jax.shard_map(shards, mesh=mesh, in_specs=in_specs, out_specs=out_specs, check_vma=False)
```

profile of v0, /device:TPU:1, one launch (start us, length us, event | category | flops | bytes accessed | tf_op | source)
XLA Modules:
  0.0 342.9 jit_solution(6629864669466501402)
XLA Ops:
  7.2 0.9 copy.17
  8.9 10.4 %all_gather.6 = bf16[16,2048]{1,0:T(8,128)(2,1)S(1)} all-gather(bf16[16,512]{1,0:T(8,128)(2,1)} %param.10), channel_id=1, replica_groups=mesh['expert'=128,'half'=4] {'half'}, dimensions={1}, use_global_device_ids=true | all-gather | bytes 81920 | tf_op jit(solution)/shard_map/all_gather | solution.py:25
  19.7 1.5 all_to_all.32
  21.2 77.1 %all_to_all.48 = bf16[128,2,2048]{2,1,0:T(2,128)(2,1)} all-to-all(bf16[128,2,2048]{2,1,0:T(2,128)(2,1)} %all_to_all.32), channel_id=1, replica_groups=mesh['expert'=128,'half'=4] {'expert'}, dimensions={0} | all-to-all | bytes 2097152 | tf_op jit(solution)/shard_map/all_to_all | solution.py:27
  98.3 1.5 all_to_all.34
  99.8 2.2 fusion.9
  102.7 1.7 convolution_convert_fusion.1
  104.5 22.2 %reduce-scatter.3.cloned.1.call-done = bf16[256,512]{1,0:T(8,128)(2,1)} async-done(((bf16[256,2048]{1,0:T(8,128)(2,1)}), bf16[256,512]{1,0:T(8,128)(2,1)}) %reduce-scatter.3.cloned.1.call-update) | async-done | bytes 262160 | tf_op jit(solution)/shard_map/reduce_scatter | solution.py:31
  126.7 1.7 all_to_all.35
  128.4 18.4 %all-to-all-start.1 = ((bf16[128,2,512]{2,1,0:T(2,128)(2,1)}), bf16[128,2,512]{2,1,0:T(2,128)(2,1)S(1)}, u32[]{:S(2)}, u32[]{:S(2)}) async-start(bf16[128,2,512]{2,1,0:T(2,128)(2,1)} %all_to_all.35), calls=%async_computation.2 | async-start | bytes 524288 | tf_op jit(solution)/shard_map/all_to_all | solution.py:34
  147.1 22.2 %all-to-all-done.1 = bf16[128,2,512]{2,1,0:T(2,128)(2,1)S(1)} async-done(((bf16[128,2,512]{2,1,0:T(2,128)(2,1)}), bf16[128,2,512]{2,1,0:T(2,128)(2,1)S(1)}, u32[]{:S(2)}, u32[]{:S(2)}) %all-to-all-start.1) | async-done | bytes 262176 | tf_op jit(solution)/shard_map/all_to_all | solution.py:34
  169.4 0.8 gather_fusion
  170.5 11.8 %psum.7 = f32[16,8,8]{2,1,0:T(8,128)S(1)} all-reduce(f32[16,8,8]{2,1,0:T(8,128)S(1)} %convolution_multiply_fusion), channel_id=1, replica_groups=mesh['expert'=128,'half'=4] {'half'}, use_global_device_ids=true, to_apply=%region_6.8 | all-reduce | flops 1024 | bytes 8192 | tf_op jit(solution)/shard_map/psum | solution.py:60
  182.6 10.1 %all_gather.7 = bf16[128,2048]{1,0:T(8,128)(2,1)S(1)} all-gather(bf16[128,512]{1,0:T(8,128)(2,1)S(1)} %fusion.13), channel_id=1, replica_groups=mesh['expert'=128,'half'=4] {'half'}, dimensions={1}, use_global_device_ids=true | all-gather | bytes 655360 | tf_op jit(solution)/shard_map/all_gather | solution.py:25
  192.7 1.1 convolution_convert_fusion
  193.8 1.5 all_to_all.38
  195.3 69.1 %all_to_all.49 = bf16[128,2,2048]{2,1,0:T(2,128)(2,1)} all-to-all(bf16[128,2,2048]{2,1,0:T(2,128)(2,1)} %all_to_all.38), channel_id=1, replica_groups=mesh['expert'=128,'half'=4] {'expert'}, dimensions={0} | all-to-all | bytes 2097152 | tf_op jit(solution)/shard_map/all_to_all | solution.py:27
  264.4 1.5 all_to_all.40
  268.7 1.8 fusion
  270.5 20.9 %reduce-scatter.5.cloned.1.call-done = bf16[256,512]{1,0:T(8,128)(2,1)} async-done(((bf16[256,2048]{1,0:T(8,128)(2,1)}), bf16[256,512]{1,0:T(8,128)(2,1)}) %reduce-scatter.5.cloned.1.call-update) | async-done | bytes 262160 | tf_op jit(solution)/shard_map/reduce_scatter | solution.py:31
  291.4 1.7 all_to_all.41
  293.2 18.7 %all-to-all-start.3 = ((bf16[128,2,512]{2,1,0:T(2,128)(2,1)}), bf16[128,2,512]{2,1,0:T(2,128)(2,1)S(1)}, u32[]{:S(2)}, u32[]{:S(2)}) async-start(bf16[128,2,512]{2,1,0:T(2,128)(2,1)} %all_to_all.41), calls=%async_computation.5 | async-start | bytes 524288 | tf_op jit(solution)/shard_map/all_to_all | solution.py:34
  312.6 21.7 %all-to-all-done.3 = bf16[128,2,512]{2,1,0:T(2,128)(2,1)S(1)} async-done(((bf16[128,2,512]{2,1,0:T(2,128)(2,1)}), bf16[128,2,512]{2,1,0:T(2,128)(2,1)S(1)}, u32[]{:S(2)}, u32[]{:S(2)}) %all-to-all-start.3) | async-done | bytes 262176 | tf_op jit(solution)/shard_map/all_to_all | solution.py:34
  334.5 0.8 gather_fusion.1
  (46 shorter events, 7.2 us)
Async XLA Ops:
  7.2 95.6 %copy-start = (bf16[1,384,2048]{2,1,0:T(8,128)(2,1)S(1)}, bf16[1,384,2048]{2,1,0:T(8,128)(2,1)}, u32[]{:S(2)}) copy-start(bf16[1,384,2048]{2,1,0:T(8,128)(2,1)} %param.17) | copy-start | bytes 4718596
  7.2 119.5 %reduce-scatter.3.cloned.1.call-start = ((), (), s32[]{:S(2)}) async-start(), calls=%async_computation.6 | async-start | bytes 1310720 | tf_op jit(solution)/shard_map/reduce_scatter | solution.py:31
  99.8 2.2 copy-start.2
  104.5 42.4 %copy-start.7 = (s32[16]{0:T(128)S(1)}, s32[16]{0:T(128)}, u32[]{:S(2)}) copy-start(s32[16]{0:T(128)} %param.14) | copy-start | bytes 196
  104.5 42.4 %copy-start.5 = (f32[16,8]{0,1:T(8,128)S(1)}, f32[16,8]{0,1:T(8,128)}, u32[]{:S(2)}) copy-start(f32[16,8]{0,1:T(8,128)} %param.13) | copy-start | bytes 1540
  104.5 42.5 %copy-start.4 = (bf16[16,512]{1,0:T(8,128)(2,1)S(1)}, bf16[16,512]{1,0:T(8,128)(2,1)}, u32[]{:S(2)}) copy-start(bf16[16,512]{1,0:T(8,128)(2,1)} %param.11) | copy-start | bytes 49156
  128.4 40.9 %all-to-all-start.1 = ((bf16[128,2,512]{2,1,0:T(2,128)(2,1)}), bf16[128,2,512]{2,1,0:T(2,128)(2,1)S(1)}, u32[]{:S(2)}, u32[]{:S(2)}) async-start(bf16[128,2,512]{2,1,0:T(2,128)(2,1)} %all_to_all.35), calls=%async_computation.2 | async-start | bytes 524288 | tf_op jit(solution)/shard_map/all_to_all | solution.py:34
  146.8 144.6 %reduce-scatter.5.cloned.1.call-start = ((), (), s32[]{:S(2)}) async-start(), calls=%async_computation.7 | async-start | bytes 1310720 | tf_op jit(solution)/shard_map/reduce_scatter | solution.py:31
  147.0 22.3 %copy-start.6 = (s32[128]{0:T(128)}, s32[128]{0:T(128)S(1)}, u32[]{:S(2)}) copy-start(s32[128]{0:T(128)S(1)} %get-tuple-element.4) | copy-start | bytes 1540
  265.9 1.4 copy-start.1
  267.3 1.4 copy-start.3
  293.2 41.2 %all-to-all-start.3 = ((bf16[128,2,512]{2,1,0:T(2,128)(2,1)}), bf16[128,2,512]{2,1,0:T(2,128)(2,1)S(1)}, u32[]{:S(2)}, u32[]{:S(2)}) async-start(bf16[128,2,512]{2,1,0:T(2,128)(2,1)} %all_to_all.41), calls=%async_computation.5 | async-start | bytes 524288 | tf_op jit(solution)/shard_map/all_to_all | solution.py:34
Sparse Core Ops, SparseCore 0:
  104.6 22.0 reduce-scatter.2
  270.6 20.7 reduce-scatter.4
where the time goes:
time: 344 us; the launch traced here: 343 us
  blocking collectives  178 us (52%)
  waiting for transfers between devices  87.1 us (25%)
  starting transfers between devices  37.2 us (11%)
  between operations  14.3 us (4%)
  local copies, waits for them, and re-layouts  13.8 us (4%)
  matrix products  9.94 us (3%)
    all_to_all x2, blocking collectives, to_experts(): lax.all_to_all(buckets, 'expert', split_axis=0, concat_axis=0, tiled=True)  146 us
    all_to_all x2, waiting for transfers between devices, to_homes(): lax.all_to_all(summed, 'expert', split_axis=0, concat_axis=0, tiled=True)  44 us
    reduce_scatter x2, waiting for transfers between devices, to_homes(): lax.psum_scatter(partial_value.astype(jnp.bfloat16), 'half', scatter_dime...  43.1 us
    all_to_all x2, starting transfers between devices, to_homes(): lax.all_to_all(summed, 'expert', split_axis=0, concat_axis=0, tiled=True)  37.1 us
    all_gather x2, blocking collectives, to_experts(): whole = lax.all_gather(items, 'half', axis=1, tiled=True)  20.5 us
    psum x1, blocking collectives, shards(): gram = lax.psum(gram_part, 'half')  11.8 us
  transfers between devices with their start and end apart: 4, of which 4 were waited for; matrix products, arithmetic and copies ran while one was open for 0% of the time, Pallas kernels for 0%

commit v1 on v0

--- a/solution.py
+++ b/solution.py
@@ -57,7 +57,7 @@
     shares = gate_probs / jnp.sum(gate_probs, axis=1, keepdims=True)
     layer_out = jnp.sum(shares[:, :, None] * out_float, axis=1).astype(jnp.bfloat16)
     gram_part = jnp.einsum("tjd,tkd->tjk", out_float, out_float) / math.sqrt(full_width)
-    gram = lax.psum(gram_part, "half")
+    gram = jnp.sum(lax.all_gather(gram_part, "half"), axis=0)
     off_diag = 1.0 - jnp.eye(top_count, dtype=jnp.float32)
     coeffs = orth_weight * gram * off_diag
     grad_out = pad_mask.astype(jnp.float32)[:, None, None] * (

time: 344 us -> 341 us (level)
    psum x1 -> x0, blocking collectives: 11.8 us -> none  [shards(): gram = lax.psum(gram_part, 'half')]
    all_gather x0 -> x1, blocking collectives: none -> 9.77 us  [shards(): gram = jnp.sum(lax.all_gather(gram_part, 'half'), axis=0)]
where the time goes in v1:
time: 341 us; the launch traced here: 340 us
  blocking collectives  176 us (52%)
  waiting for transfers between devices  87.1 us (26%)
  starting transfers between devices  37.2 us (11%)
  between operations  14.3 us (4%)
  local copies, waits for them, and re-layouts  13.8 us (4%)
  matrix products  9.93 us (3%)
    all_to_all x2, blocking collectives, to_experts(): lax.all_to_all(buckets, 'expert', split_axis=0, concat_axis=0, tiled=True)  145 us
    all_to_all x2, waiting for transfers between devices, to_homes(): lax.all_to_all(summed, 'expert', split_axis=0, concat_axis=0, tiled=True)  44 us
    reduce_scatter x2, waiting for transfers between devices, to_homes(): lax.psum_scatter(partial_value.astype(jnp.bfloat16), 'half', scatter_dime...  43.1 us
    all_to_all x2, starting transfers between devices, to_homes(): lax.all_to_all(summed, 'expert', split_axis=0, concat_axis=0, tiled=True)  37.1 us
    all_gather x2, blocking collectives, to_experts(): whole = lax.all_gather(items, 'half', axis=1, tiled=True)  21.1 us
    all_gather x1, blocking collectives, shards(): gram = jnp.sum(lax.all_gather(gram_part, 'half'), axis=0)  9.77 us
  transfers between devices with their start and end apart: 4, of which 4 were waited for; matrix products, arithmetic and copies ran while one was open for 0% of the time, Pallas kernels for 0%

profile of v1, /device:TPU:1, one launch (start us, length us, event | category | flops | bytes accessed | tf_op | source)
XLA Modules:
  0.0 340.1 jit_solution(17590888926644102155)
XLA Ops:
  7.2 0.9 copy.20
  8.9 10.4 %all_gather.12 = bf16[16,2048]{1,0:T(8,128)(2,1)S(1)} all-gather(bf16[16,512]{1,0:T(8,128)(2,1)} %param.10), channel_id=1, replica_groups=mesh['expert'=128,'half'=4] {'half'}, dimensions={1}, use_global_device_ids=true | all-gather | bytes 81920 | tf_op jit(solution)/shard_map/all_gather | solution.py:25
  19.7 1.5 all_to_all.32
  21.2 77.1 %all_to_all.48 = bf16[128,2,2048]{2,1,0:T(2,128)(2,1)} all-to-all(bf16[128,2,2048]{2,1,0:T(2,128)(2,1)} %all_to_all.32), channel_id=1, replica_groups=mesh['expert'=128,'half'=4] {'expert'}, dimensions={0} | all-to-all | bytes 2097152 | tf_op jit(solution)/shard_map/all_to_all | solution.py:27
  98.3 1.5 all_to_all.34
  99.8 2.2 fusion.9
  102.7 1.7 convolution_convert_fusion.1
  104.5 22.2 %reduce-scatter.3.cloned.1.call-done = bf16[256,512]{1,0:T(8,128)(2,1)} async-done(((bf16[256,2048]{1,0:T(8,128)(2,1)}), bf16[256,512]{1,0:T(8,128)(2,1)}) %reduce-scatter.3.cloned.1.call-update) | async-done | bytes 262160 | tf_op jit(solution)/shard_map/reduce_scatter | solution.py:31
  126.7 1.7 all_to_all.35
  128.4 18.4 %all-to-all-start.1 = ((bf16[128,2,512]{2,1,0:T(2,128)(2,1)}), bf16[128,2,512]{2,1,0:T(2,128)(2,1)S(1)}, u32[]{:S(2)}, u32[]{:S(2)}) async-start(bf16[128,2,512]{2,1,0:T(2,128)(2,1)} %all_to_all.35), calls=%async_computation.2 | async-start | bytes 524288 | tf_op jit(solution)/shard_map/all_to_all | solution.py:34
  147.1 22.2 %all-to-all-done.1 = bf16[128,2,512]{2,1,0:T(2,128)(2,1)S(1)} async-done(((bf16[128,2,512]{2,1,0:T(2,128)(2,1)}), bf16[128,2,512]{2,1,0:T(2,128)(2,1)S(1)}, u32[]{:S(2)}, u32[]{:S(2)}) %all-to-all-start.1) | async-done | bytes 262176 | tf_op jit(solution)/shard_map/all_to_all | solution.py:34
  169.4 0.8 gather_fusion
  170.5 9.8 %all-gather = f32[64,8,8]{2,1,0:T(8,128)S(1)} all-gather(f32[16,8,8]{2,1,0:T(8,128)S(1)} %convolution_multiply_fusion), channel_id=2, replica_groups=mesh['expert'=128,'half'=4] {'half'}, dimensions={0}, use_global_device_ids=true | all-gather | bytes 20480 | tf_op jit(solution)/shard_map/all_gather | solution.py:60
  180.5 10.7 %all_gather.15 = bf16[128,2048]{1,0:T(8,128)(2,1)S(1)} all-gather(bf16[128,512]{1,0:T(8,128)(2,1)S(1)} %fusion.13), channel_id=1, replica_groups=mesh['expert'=128,'half'=4] {'half'}, dimensions={1}, use_global_device_ids=true | all-gather | bytes 655360 | tf_op jit(solution)/shard_map/all_gather | solution.py:25
  191.3 1.1 convolution_convert_fusion
  192.4 1.5 all_to_all.38
  193.9 67.8 %all_to_all.49 = bf16[128,2,2048]{2,1,0:T(2,128)(2,1)} all-to-all(bf16[128,2,2048]{2,1,0:T(2,128)(2,1)} %all_to_all.38), channel_id=1, replica_groups=mesh['expert'=128,'half'=4] {'expert'}, dimensions={0} | all-to-all | bytes 2097152 | tf_op jit(solution)/shard_map/all_to_all | solution.py:27
  261.7 1.5 all_to_all.40
  266.0 1.8 fusion
  267.7 20.9 %reduce-scatter.5.cloned.1.call-done = bf16[256,512]{1,0:T(8,128)(2,1)} async-done(((bf16[256,2048]{1,0:T(8,128)(2,1)}), bf16[256,512]{1,0:T(8,128)(2,1)}) %reduce-scatter.5.cloned.1.call-update) | async-done | bytes 262160 | tf_op jit(solution)/shard_map/reduce_scatter | solution.py:31
  288.6 1.7 all_to_all.41
  290.3 18.8 %all-to-all-start.3 = ((bf16[128,2,512]{2,1,0:T(2,128)(2,1)}), bf16[128,2,512]{2,1,0:T(2,128)(2,1)S(1)}, u32[]{:S(2)}, u32[]{:S(2)}) async-start(bf16[128,2,512]{2,1,0:T(2,128)(2,1)} %all_to_all.41), calls=%async_computation.5 | async-start | bytes 524288 | tf_op jit(solution)/shard_map/all_to_all | solution.py:34
  309.9 21.7 %all-to-all-done.3 = bf16[128,2,512]{2,1,0:T(2,128)(2,1)S(1)} async-done(((bf16[128,2,512]{2,1,0:T(2,128)(2,1)}), bf16[128,2,512]{2,1,0:T(2,128)(2,1)S(1)}, u32[]{:S(2)}, u32[]{:S(2)}) %all-to-all-start.3) | async-done | bytes 262176 | tf_op jit(solution)/shard_map/all_to_all | solution.py:34
  331.7 0.8 gather_fusion.1
  (47 shorter events, 7.2 us)
Async XLA Ops:
  7.2 95.6 %copy-start = (bf16[1,384,2048]{2,1,0:T(8,128)(2,1)S(1)}, bf16[1,384,2048]{2,1,0:T(8,128)(2,1)}, u32[]{:S(2)}) copy-start(bf16[1,384,2048]{2,1,0:T(8,128)(2,1)} %param.17) | copy-start | bytes 4718596
  7.2 119.5 %reduce-scatter.3.cloned.1.call-start = ((), (), s32[]{:S(2)}) async-start(), calls=%async_computation.6 | async-start | bytes 1310720 | tf_op jit(solution)/shard_map/reduce_scatter | solution.py:31
  99.8 2.2 copy-start.2
  104.5 42.4 %copy-start.7 = (s32[16]{0:T(128)S(1)}, s32[16]{0:T(128)}, u32[]{:S(2)}) copy-start(s32[16]{0:T(128)} %param.14) | copy-start | bytes 196
  104.5 42.4 %copy-start.5 = (f32[16,8]{0,1:T(8,128)S(1)}, f32[16,8]{0,1:T(8,128)}, u32[]{:S(2)}) copy-start(f32[16,8]{0,1:T(8,128)} %param.13) | copy-start | bytes 1540
  104.5 42.5 %copy-start.4 = (bf16[16,512]{1,0:T(8,128)(2,1)S(1)}, bf16[16,512]{1,0:T(8,128)(2,1)}, u32[]{:S(2)}) copy-start(bf16[16,512]{1,0:T(8,128)(2,1)} %param.11) | copy-start | bytes 49156
  128.4 40.9 %all-to-all-start.1 = ((bf16[128,2,512]{2,1,0:T(2,128)(2,1)}), bf16[128,2,512]{2,1,0:T(2,128)(2,1)S(1)}, u32[]{:S(2)}, u32[]{:S(2)}) async-start(bf16[128,2,512]{2,1,0:T(2,128)(2,1)} %all_to_all.35), calls=%async_computation.2 | async-start | bytes 524288 | tf_op jit(solution)/shard_map/all_to_all | solution.py:34
  146.8 141.8 %reduce-scatter.5.cloned.1.call-start = ((), (), s32[]{:S(2)}) async-start(), calls=%async_computation.7 | async-start | bytes 1310720 | tf_op jit(solution)/shard_map/reduce_scatter | solution.py:31
  147.0 22.3 %copy-start.6 = (s32[128]{0:T(128)}, s32[128]{0:T(128)S(1)}, u32[]{:S(2)}) copy-start(s32[128]{0:T(128)S(1)} %get-tuple-element.4) | copy-start | bytes 1540
  263.1 1.4 copy-start.1
  264.5 1.4 copy-start.3
  290.3 41.3 %all-to-all-start.3 = ((bf16[128,2,512]{2,1,0:T(2,128)(2,1)}), bf16[128,2,512]{2,1,0:T(2,128)(2,1)S(1)}, u32[]{:S(2)}, u32[]{:S(2)}) async-start(bf16[128,2,512]{2,1,0:T(2,128)(2,1)} %all_to_all.41), calls=%async_computation.5 | async-start | bytes 524288 | tf_op jit(solution)/shard_map/all_to_all | solution.py:34
Sparse Core Ops, SparseCore 0:
  104.6 22.0 reduce-scatter.2
  267.8 20.7 reduce-scatter.4
